TPU v7x, 128 devices: a whole 4x4x4 slice. The times are simulated.
128 devices in a mesh: section: 16 (over z_lo, x, core), tp: 8 (over y, z_hi).
Axes of the slice: x: 4, y: 4, z: 4 (z_hi: 2, z_lo: 2; z = z_hi * 2 + z_lo), core: 2. Of those that a mesh axis runs over, the one named last changes fastest.
Arguments:
- tokens: bfloat16 [16, 256, 4096], P('section', None, 'tp'), may hold values from -96 to 96
- cotangent: bfloat16 [16, 256, 4096], P('section', None, 'tp'), may hold values from -6 to 6
- memory: bfloat16 [1024, 4096], P('section', 'tp'), may hold values from -12 to 12
- w_query: bfloat16 [16, 4096, 4096], P('section', None, 'tp'), may hold values from -0.1875 to 0.1875
- w_key: bfloat16 [16, 4096, 4096], P('section', None, 'tp'), may hold values from -0.1875 to 0.1875
- w_value: bfloat16 [16, 4096, 4096], P('section', None, 'tp'), may hold values from -0.09375 to 0.09375
- w_out: bfloat16 [16, 4096, 4096], P('section', 'tp'), may hold values from -0.09375 to 0.09375
Outputs:
- attended_out: bfloat16 [16, 256, 4096], P('section', None, 'tp')
- grad_tokens: bfloat16 [16, 256, 4096], P('section', None, 'tp')
- grad_memory: bfloat16 [1024, 4096], P('section', 'tp')
All inputs are finite; a program needn't handle non-finite values.
Results may differ from a plain program's by a relative error of at most 0.02.
Values may be sent and summed in bfloat16 or wider, within the bound.
A program may use at most 128 MiB of HBM per device.

v0:
```python
import jax
import jax.numpy as jnp
from jax import lax
from jax.sharding import PartitionSpec as P

HEAD_SIZE = 256


def on_device(tokens, cotangent, memory, w_query, w_key, w_value, w_out):
    score_scale = HEAD_SIZE ** (-0.5)
    inner_local = w_query.shape[2]
    heads_local = inner_local // HEAD_SIZE
    own_rows = memory.shape[0]
    own_cols = memory.shape[1]
    target, grad_out = (
        lax.all_gather(tokens[0], "tp", axis=1, tiled=True),
        lax.all_gather(cotangent[0], "tp", axis=1, tiled=True),
    )
    rows_target = target.shape[0]
    wq_layer = w_query[0]
    wk_layer = w_key[0]
    wv_layer = w_value[0]
    wo_layer = w_out[0]
    section_rows = lax.all_gather(memory, "tp", axis=1, tiled=True)
    piece = lax.all_gather(section_rows, "section", axis=0, tiled=True)
    key_part = jnp.dot(piece, wk_layer, preferred_element_type=jnp.float32).astype(jnp.bfloat16)
    value_part = jnp.dot(piece, wv_layer, preferred_element_type=jnp.float32).astype(jnp.bfloat16)
    joined = jnp.stack([key_part, value_part], axis=0)
    keys = joined[0]
    values = joined[1]
    rows_memory = keys.shape[0]
    key_per_head = keys.reshape(rows_memory, heads_local, HEAD_SIZE)
    value_per_head = values.reshape(rows_memory, heads_local, HEAD_SIZE)
    queries = jnp.dot(target, wq_layer, preferred_element_type=jnp.float32).astype(jnp.bfloat16)
    query_per_head = queries.reshape(rows_target, heads_local, HEAD_SIZE)
    attention_scores = (
        jnp.einsum("iws,jws->wij", query_per_head, key_per_head, preferred_element_type=jnp.float32)
        * score_scale
    )
    top = jnp.max(attention_scores, axis=-1, keepdims=True)
    weights = jnp.exp(attention_scores - top)
    probs = weights / jnp.sum(weights, axis=-1, keepdims=True)
    probabilities_batch = probs.astype(jnp.bfloat16)
    context_output = jnp.einsum(
        "crb,bcl->rcl", probabilities_batch, value_per_head, preferred_element_type=jnp.float32
    )
    context_output = context_output.astype(jnp.bfloat16).reshape(rows_target, inner_local)
    out_terms = jnp.dot(context_output, wo_layer, preferred_element_type=jnp.float32)
    attended = lax.psum_scatter(
        out_terms.astype(jnp.bfloat16), "tp", scatter_dimension=1, tiled=True
    )
    grad_context = jnp.einsum(
        "td,kd->tk", grad_out, wo_layer, preferred_element_type=jnp.float32
    ).astype(jnp.bfloat16)
    gradient_heads = grad_context.reshape(rows_target, heads_local, HEAD_SIZE)
    probability_gradient = jnp.einsum(
        "iws,jws->wij", gradient_heads, value_per_head, preferred_element_type=jnp.float32
    )
    delta = jnp.sum(probability_gradient * probs, axis=-1, keepdims=True)
    value_gradient = jnp.einsum(
        "cry,rcs->ycs", probabilities_batch, gradient_heads, preferred_element_type=jnp.float32
    ).astype(jnp.bfloat16)
    score_gradient = (probs * (probability_gradient - delta) * score_scale).astype(jnp.bfloat16)
    query_gradient = jnp.einsum(
        "crb,bcl->rcl", score_gradient, key_per_head, preferred_element_type=jnp.float32
    ).astype(jnp.bfloat16)
    key_gradient = jnp.einsum(
        "cry,rcs->ycs", score_gradient, query_per_head, preferred_element_type=jnp.float32
    ).astype(jnp.bfloat16)
    query_gradient = query_gradient.reshape(rows_target, inner_local)
    target_terms = jnp.einsum(
        "tk,dk->td", query_gradient, wq_layer, preferred_element_type=jnp.float32
    )
    grad_target = lax.psum_scatter(
        target_terms.astype(jnp.bfloat16), "tp", scatter_dimension=1, tiled=True
    )
    key_grad_rows = key_gradient.reshape(rows_memory, inner_local)
    value_grad_rows = value_gradient.reshape(rows_memory, inner_local)
    tp_count = lax.axis_size("tp")
    section_count = rows_memory // own_rows
    key_blocks = key_grad_rows.reshape(section_count, own_rows, inner_local)
    value_blocks = value_grad_rows.reshape(section_count, own_rows, inner_local)
    key_weight_blocks = wk_layer.reshape(tp_count, own_cols, inner_local)
    value_weight_blocks = wv_layer.reshape(tp_count, own_cols, inner_local)
    block_terms = jnp.einsum(
        "smk,tdk->stmd", key_blocks, key_weight_blocks, preferred_element_type=jnp.float32
    )
    block_terms = block_terms + jnp.einsum(
        "smk,tdk->stmd", value_blocks, value_weight_blocks, preferred_element_type=jnp.float32
    )
    block_terms = block_terms.reshape(section_count * tp_count * own_rows, own_cols)
    grad_mem = lax.psum_scatter(block_terms, ("section", "tp"), scatter_dimension=0, tiled=True)
    return (attended[None], grad_target[None], grad_mem.astype(jnp.bfloat16))


def solution(mesh):
    placed = (
        P("section", None, "tp"),
        P("section", None, "tp"),
        P("section", "tp"),
        P("section", None, "tp"),
        P("section", None, "tp"),
        P("section", None, "tp"),
        P("section", "tp", None),
    )
    return jax.shard_map(
        on_device,
        mesh=mesh,
        in_specs=placed,
        out_specs=(P("section", None, "tp"), P("section", None, "tp"), P("section", "tp")),
        check_vma=False,
    )
```

profile of v0, /device:TPU:1, one launch (start us, length us, event | category | flops | bytes accessed | tf_op | source)
XLA Modules:
  0.0 1083.5 jit_solution(17411626067912658002)
XLA Ops:
  7.2 0.0 all-gather.8.cloned.1.call-start
  7.2 0.7 all-gather.8.cloned.1.call-update
  7.9 0.0 all-gather.10.cloned.1.call-start
  7.9 0.7 all-gather.10.cloned.1.call-update
  8.6 0.0 all-gather.6.cloned.1.call-start
  8.7 33.3 %all_gather.12 = bf16[64,4096]{1,0:T(8,128)(2,1)} all-gather(bf16[64,512]{1,0:T(8,128)(2,1)} %param.9), channel_id=1, replica_groups=mesh['section'=16,'tp'=8] {'tp'}, dimensions={1}, use_global_device_ids=true | all-gather | bytes 589824 | tf_op jit(solution)/shard_map/all_gather | solution.py:24
  42.0 0.0 all-gather.6.cloned.1.call-update
  42.0 0.0 reduce-scatter.8.cloned.1.call-start
  42.0 28.2 %all-gather.8.cloned.1.call-done = bf16[1,256,4096]{2,1,0:T(8,128)(2,1)} async-done(((bf16[1,256,512]{2,1,0:T(8,128)(2,1)}), bf16[1,256,4096]{2,1,0:T(8,128)(2,1)}) %all-gather.8.cloned.1.call-update) | async-done | bytes 2097168 | tf_op jit(solution)/shard_map/all_gather | solution.py:16
  70.2 4.1 fusion.40
  74.3 0.8 copy.30
  75.1 53.9 %all-gather.10.cloned.1.call-done = bf16[1,256,4096]{2,1,0:T(8,128)(2,1)} async-done(((bf16[1,256,512]{2,1,0:T(8,128)(2,1)}), bf16[1,256,4096]{2,1,0:T(8,128)(2,1)}) %all-gather.10.cloned.1.call-update) | async-done | bytes 2097168 | tf_op jit(solution)/shard_map/all_gather | solution.py:17
  129.0 4.1 fusion.45
  133.2 0.1 copy.31
  133.3 49.6 %all-gather.6.cloned.1.call-done = bf16[1024,4096]{1,0:T(8,128)(2,1)} async-done(((bf16[64,4096]{1,0:T(8,128)(2,1)}), bf16[1024,4096]{1,0:T(8,128)(2,1)}) %all-gather.6.cloned.1.call-update) | async-done | bytes 8388624 | tf_op jit(solution)/shard_map/all_gather | solution.py:25
  182.9 0.0 copy-start.3
  182.9 0.0 copy-start.4
  182.9 9.2 fusion.27
  192.1 0.5 fusion.66
  192.6 0.0 copy-done.3
  192.6 0.0 copy-done.4
  192.6 0.0 copy-start.2
  192.6 5.6 fusion.30
  198.3 3.6 fusion.65
  201.9 3.1 fusion.36
  205.0 0.0 copy-done.2
  205.0 5.8 fusion.33
  210.8 2.5 copy.25
  213.3 0.7 reshape.33
  214.0 2.5 copy.23
  216.5 1.5 reshape.31
  218.0 0.0 copy-start
  218.0 12.9 %fusion.51 = f32[16,64,8,512]{3,1,2,0:T(8,128)} fusion(bf16[8,512,512,1]{2,1,0,3:T(8,128)(2,1)} %bitcast.89, bf16[16,64,512,1]{2,1,0,3:T(8,128)(2,1)} %reshape.31), kind=kOutput, calls=%fused_computation.36 | convolution fusion | flops 4294967296 | bytes 22020096 | tf_op jit(solution)/shard_map/smk,tdk->stmd/dot_general | solution.py:85
  230.9 0.0 copy-done
  230.9 11.8 %convolution_add_fusion = f32[16,64,8,512]{3,1,2,0:T(8,128)} fusion(f32[16,64,8,512]{3,1,2,0:T(8,128)} %fusion.51, bf16[8,512,512,1]{2,1,0,3:T(8,128)(2,1)S(1)} %bitcast.80, bf16[16,64,512,1]{2,1,0,3:T(8,128)(2,1)S(1)} %reshape.33), kind=kOutput, calls=%fused_computation.2 | convolution fusion | flops 4299161600 | bytes 38797312 | tf_op jit(solution)/shard_map/smk,tdk->stmd/dot_general | solution.py:88
  242.7 0.0 copy-start.5
  242.7 0.0 reduce-scatter.8.cloned.1.call-update
  242.7 0.0 reduce-scatter.6.cloned.1.call-start
  242.8 1.1 copy-done.5
  243.9 5.7 fusion.37
  249.7 4.8 convolution_convert_fusion
  254.5 0.0 copy-start.6
  254.5 0.0 reduce-scatter.6.cloned.1.call-update
  254.5 0.0 reduce-scatter.4.cloned.1.call-start
  254.5 1.5 copy-done.6
  256.0 0.0 copy-start.1
  256.0 0.6 convolution_convert_fusion.3
  256.6 1.6 copy-done.1
  258.2 2.6 convolution_convert_fusion.1
  260.9 0.0 reduce-scatter.4.cloned.1.call-update
  260.9 656.6 %reduce-scatter.8.cloned.1.call-done = f32[64,512]{1,0:T(8,128)} async-done(((f32[8192,512]{1,0:T(8,128)}), f32[64,512]{1,0:T(8,128)}) %reduce-scatter.8.cloned.1.call-update) | async-done | bytes 131088 | tf_op jit(solution)/shard_map/reduce_scatter | solution.py:92
  917.6 1.5 convert_element_type.67
  919.1 78.8 %reduce-scatter.6.cloned.1.call-done = bf16[256,512]{1,0:T(8,128)(2,1)} async-done(((bf16[256,4096]{1,0:T(8,128)(2,1)}), bf16[256,512]{1,0:T(8,128)(2,1)}) %reduce-scatter.6.cloned.1.call-update) | async-done | bytes 262160 | tf_op jit(solution)/shard_map/reduce_scatter | solution.py:74
  997.9 78.7 %reduce-scatter.4.cloned.1.call-done = bf16[256,512]{1,0:T(8,128)(2,1)} async-done(((bf16[256,4096]{1,0:T(8,128)(2,1)}), bf16[256,512]{1,0:T(8,128)(2,1)}) %reduce-scatter.4.cloned.1.call-update) | async-done | bytes 262160 | tf_op jit(solution)/shard_map/reduce_scatter | solution.py:49
Async XLA Ops:
  7.2 63.0 %all-gather.8.cloned.1.call-start = ((), (), s32[]{:S(2)}) async-start(), calls=%async_computation.7 | async-start | bytes 2359296 | tf_op jit(solution)/shard_map/all_gather | solution.py:16
  7.9 121.1 %all-gather.10.cloned.1.call-start = ((), (), s32[]{:S(2)}) async-start(), calls=%async_computation.8 | async-start | bytes 2359296 | tf_op jit(solution)/shard_map/all_gather | solution.py:17
  8.6 174.2 %all-gather.6.cloned.1.call-start = ((), (), s32[]{:S(2)}) async-start(), calls=%async_computation.3 | async-start | bytes 8912896 | tf_op jit(solution)/shard_map/all_gather | solution.py:25
  42.0 875.6 %reduce-scatter.8.cloned.1.call-start = ((), (), s32[]{:S(2)}) async-start(), calls=%async_computation.6 | async-start | bytes 16908288 | tf_op jit(solution)/shard_map/reduce_scatter | solution.py:92
  182.9 9.8 copy-start.3
  182.9 9.8 copy-start.4
  192.6 12.4 %copy-start.2 = (f32[2,256,1024]{2,1,0:T(8,128)}, f32[2,256,1024]{2,1,0:T(8,128)S(1)}, u32[]{:S(2)}) copy-start(f32[2,256,1024]{2,1,0:T(8,128)S(1)} %fusion.66) | copy-start | bytes 6291460
  218.0 12.9 %copy-start = (bf16[1,4096,512]{2,1,0:T(8,128)(2,1)S(1)}, bf16[1,4096,512]{2,1,0:T(8,128)(2,1)}, u32[]{:S(2)}) copy-start(bf16[1,4096,512]{2,1,0:T(8,128)(2,1)} %param.12) | copy-start | bytes 12582916
  242.7 1.2 copy-start.5
  242.7 755.2 %reduce-scatter.6.cloned.1.call-start = ((), (), s32[]{:S(2)}) async-start(), calls=%async_computation.5 | async-start | bytes 2359296 | tf_op jit(solution)/shard_map/reduce_scatter | solution.py:74
  254.5 1.6 copy-start.6
  254.5 822.1 %reduce-scatter.4.cloned.1.call-start = ((), (), s32[]{:S(2)}) async-start(), calls=%async_computation.4 | async-start | bytes 2359296 | tf_op jit(solution)/shard_map/reduce_scatter | solution.py:49
  256.0 2.2 copy-start.1
Sparse Core Ops, SparseCore 0:
  10.2 59.9 all-gather.7
  72.4 56.6 all-gather.9
  130.7 52.0 all-gather.5
  242.8 674.6 reduce-scatter.7
  921.8 76.1 reduce-scatter.5
  1002.6 73.9 reduce-scatter.3
where the time goes:
time: 1080 us
  waiting for transfers between devices  947 us (88%)
  matrix products  74.5 us (7%)
  blocking collectives  33.3 us (3%)
  between operations  14.2 us (1%)
  local copies, waits for them, and re-layouts  12.5 us (1%)
    reduce_scatter x1, waiting for transfers between devices, on_device(): lax.psum_scatter(block_terms, ('section', 'tp'), scatter_dimension=0, til...  657 us
    reduce_scatter x1, waiting for transfers between devices, on_device(): lax.psum_scatter(target_terms.astype(jnp.bfloat16), 'tp', scatter_dimensi...  78.8 us
    reduce_scatter x1, waiting for transfers between devices, on_device(): lax.psum_scatter(out_terms.astype(jnp.bfloat16), 'tp', scatter_dimension=...  78.7 us
    all_gather x1, waiting for transfers between devices, on_device(): lax.all_gather(cotangent[0], 'tp', axis=1, tiled=True)  53.9 us
    all_gather x1, waiting for transfers between devices, on_device(): piece = lax.all_gather(section_rows, 'section', axis=0, tiled=True)  49.6 us
    all_gather x1, blocking collectives, on_device(): section_rows = lax.all_gather(memory, 'tp', axis=1, tiled=True)  33.3 us
    all_gather x1, waiting for transfers between devices, on_device(): lax.all_gather(tokens[0], 'tp', axis=1, tiled=True)  28.2 us
  transfers between devices with their start and end apart: 6, of which 6 were waited for; matrix products, arithmetic and copies ran while one was open for 2% of the time, Pallas kernels for 0%

commit v1 on v0

v1 whole, which is shorter than its diff:
```python
import functools

import jax
import jax.numpy as jnp
from jax import lax
from jax.experimental import pallas as pl
from jax.experimental.pallas import tpu as pltpu
from jax.sharding import PartitionSpec as P

HEAD_SIZE = 256
HEADS = 2
FEATURES = 512
D = 4096
TARGETS = 256
MEMORY = 1024
OWN_ROWS = 64
SIDE = 2048
SCALE = HEAD_SIZE ** -0.5
BF16 = jnp.bfloat16
F32 = jnp.float32
N_SEMS = 128
N_LOCAL = 48


def dot(a, b):
    return lax.dot_general(a, b, (((1,), (0,)), ((), ())), preferred_element_type=F32)


def dot_nt(a, b):
    return lax.dot_general(a, b, (((1,), (1,)), ((), ())), preferred_element_type=F32)


def dot_tn(a, b):
    return lax.dot_general(a, b, (((0,), (0,)), ((), ())), preferred_element_type=F32)


def aligned(start, size):
    return pl.ds(pl.multiple_of(start, size), size)


def add_rows(dst, srcs):
    rows = dst.shape[0]

    def step(i, _):
        part = aligned(i * 16, 16)
        total = srcs[0][part, :].astype(F32)
        for src in srcs[1:]:
            total = total + src[part, :].astype(F32)
        dst[part, :] = total.astype(dst.dtype)
        return 0

    lax.fori_loop(0, rows // 16, step, 0)


def kernel(
    tokens, cotangent, memory, w_query, w_key, w_value, w_out,
    attended, grad_tokens, grad_memory,
    wkv, wq, wo, mem, tok, cot, kv, gkv, queries, gctx, ctx, gq, probs, probs_b, dscores,
    core_in, relay_in, final_in, z_in, y_in, att_in, att_z, tgt_in, tgt_z,
    send_sem, recv_sem, local_sem,
):
    section = lax.axis_index("section")
    tp = lax.axis_index("tp")
    c = lax.rem(section, 2)
    x = lax.rem(section // 2, 4)
    y = tp // 2
    zh = lax.rem(tp, 2)
    z = zh * 2 + section // 8

    def device(dx=0, dy=0, dz=0, dc=0):
        to_x, to_y, to_z = lax.rem(x + dx, 4), lax.rem(y + dy, 4), lax.rem(z + dz, 4)
        to_c = lax.rem(c + dc, 2)
        return ((lax.rem(to_z, 2) * 4 + to_x) * 2 + to_c, to_y * 2 + to_z // 2)

    counter = [0, 0]
    sends = []

    def remote(src, dst, where):
        i = counter[0]
        counter[0] += 1
        copy = pltpu.make_async_remote_copy(
            src_ref=src, dst_ref=dst, send_sem=send_sem.at[i], recv_sem=recv_sem.at[i],
            device_id=device(**where), device_id_type=pl.DeviceIdType.MESH,
        )
        copy.start()
        sends.append(copy)
        return copy

    def local(src, dst):
        i = counter[1]
        counter[1] += 1
        copy = pltpu.make_async_copy(src, dst, local_sem.at[i])
        copy.start()
        return copy

    def flush():
        for copy in sends:
            copy.wait_send()
        sends.clear()

    XP, XM, YP, YM = dict(dx=1), dict(dx=3), dict(dy=1), dict(dy=3)
    CORE, ZFAR = dict(dc=1), dict(dz=2)

    def x_at(dx):
        return lax.rem(x + dx, 4)

    def side(high):
        return aligned(high * SIDE, SIDE)

    def piece(dx, core, dz, half=None):
        to_z = lax.rem(z + dz, 4)
        row = core * 128 + lax.rem(to_z, 2) * 64
        rows = aligned(row, 64) if half is None else aligned(row + half * 32, 32)
        return mem.at[x_at(dx), rows, side(to_z // 2)]

    def block(buf, high, dy):
        return buf.at[:, aligned(high * SIDE + lax.rem(y + dy, 4) * FEATURES, FEATURES)]

    own_mem = mem.at[x, aligned(c * 128 + lax.rem(z, 2) * 64, 64), aligned(zh * SIDE + y * FEATURES, FEATURES)]
    near, far = zh, 1 - zh

    mem_load = local(memory, own_mem)
    tok_load = local(tokens.at[0], block(tok, near, 0))
    cot_load = local(cotangent.at[0], block(cot, near, 0))
    kv_loads, q_loads, o_loads = [], [], []
    for high in range(2):
        for row in range(4):
            src = pl.ds((row * 2 + high) * FEATURES, FEATURES)
            dst = pl.ds(high * SIDE + row * FEATURES, FEATURES)
            kv_loads.append(local(w_key.at[0, src, :], wkv.at[dst, pl.ds(0, FEATURES)]))
            kv_loads.append(local(w_value.at[0, src, :], wkv.at[dst, pl.ds(FEATURES, FEATURES)]))
    for high in range(2):
        for row in range(4):
            src = pl.ds((row * 2 + high) * FEATURES, FEATURES)
            dst = pl.ds(high * SIDE + row * FEATURES, FEATURES)
            q_loads.append(local(w_query.at[0, src, :], wq.at[dst, :]))
            o_loads.append(local(w_out.at[0, :, src], wo.at[:, dst]))

    barrier = pltpu.get_barrier_semaphore()
    peers = [XP, XM, YP, YM, dict(dy=2), dict(dz=1), dict(dz=3), ZFAR, CORE]
    for where in peers:
        pl.semaphore_signal(barrier, inc=1, device_id=device(**where), device_id_type=pl.DeviceIdType.MESH)
    pl.semaphore_wait(barrier, len(peers))

    mem_y = [remote(memory, own_mem, dict(dy=dy)) for dy in (1, 3, 2)]
    mem_load.wait()
    for copy in mem_y:
        copy.wait_recv()
    own = piece(0, c, 0)
    right, left, core_own = {}, {}, {}
    mem_z = {}

    def spread(dz):
        right[dz] = remote(piece(0, c, dz), piece(0, c, dz), XP)
        left[dz] = remote(piece(0, c, dz), piece(0, c, dz), XM)
        core_own[dz] = remote(piece(0, c, dz), piece(0, c, dz), CORE)

    right[0] = remote(own, own, XP)
    left[0] = remote(own, own, XM)
    for dz in (1, 3, 2):
        mem_z[dz] = remote(own, own, dict(dz=dz))
    core_own[0] = remote(own, own, CORE)

    def spread_targets(high, from_hbm):
        t = tokens.at[0] if from_hbm else block(tok, high, 0)
        g = cotangent.at[0] if from_hbm else block(cot, high, 0)
        t_dst, g_dst = block(tok, high, 0), block(cot, high, 0)
        t_right = remote(t, t_dst, YP)
        g_left = remote(g, g_dst, YM)
        g_right = remote(g, g_dst, YP)
        t_left = remote(t, t_dst, YM)
        return t_right, g_left, g_right, t_left

    near_ring = spread_targets(near, True)
    core_right, core_left, core_opposite = {}, {}, {}
    on_right, on_left = {}, {}

    def arrive_x(dz):
        right[dz].wait_recv()
        on_right[dz] = remote(piece(3, c, dz, 0), piece(3, c, dz, 0), XP)
        core_left[dz] = remote(piece(3, c, dz), piece(3, c, dz), CORE)
        left[dz].wait_recv()
        on_left[dz] = remote(piece(1, c, dz, 1), piece(1, c, dz, 1), XM)
        core_right[dz] = remote(piece(1, c, dz), piece(1, c, dz), CORE)

    def forward_targets(high, ring):
        t_right, g_left, g_right, t_left = ring
        t_right.wait_recv()
        t_on = remote(block(tok, high, 3), block(tok, high, 3), YP)
        g_left.wait_recv()
        g_on = remote(block(cot, high, 1), block(cot, high, 1), YM)
        return t_on, g_on

    def keys_values(dx):
        to_x = x_at(dx)
        rows = aligned(to_x * 256, 256)

        def step(n, _):
            cols = aligned(n * 256, 256)
            kv[rows, cols] = dot(mem[to_x], wkv[:, cols]).astype(BF16)
            return 0

        lax.fori_loop(0, 4, step, 0)

    arrive_x(0)
    for dz in (1, 3, 2):
        mem_z[4 - dz].wait_recv()
        spread(dz)
    tok_z = remote(tokens.at[0], block(tok, near, 0), ZFAR)
    cot_z = remote(cotangent.at[0], block(cot, near, 0), ZFAR)
    near_on = forward_targets(near, near_ring)
    for copy in kv_loads:
        copy.wait()
    for dz in (0, 1, 3, 2):
        core_own[dz].wait_recv()
    keys_values(0)
    arrive_x(1)
    arrive_x(3)
    tok_z.wait_recv()
    cot_z.wait_recv()
    far_ring = spread_targets(far, False)
    arrive_x(2)
    far_on = forward_targets(far, far_ring)

    def arrive_opposite(dz):
        on_right[dz].wait_recv()
        a = remote(piece(2, c, dz, 0), piece(2, c, dz, 0), CORE)
        on_left[dz].wait_recv()
        b = remote(piece(2, c, dz, 1), piece(2, c, dz, 1), CORE)
        core_opposite[dz] = (a, b)

    for dz in (0, 1):
        arrive_opposite(dz)
    for dz in (0, 1, 3, 2):
        core_right[dz].wait_recv()
    keys_values(1)
    for dz in (0, 1, 3, 2):
        core_left[dz].wait_recv()
    keys_values(3)
    for dz in (3, 2):
        arrive_opposite(dz)

    for ring, on in ((near_ring, near_on), (far_ring, far_on)):
        t_right, g_left, g_right, t_left = ring
        g_right.wait_recv()
        t_left.wait_recv()
        on[0].wait_recv()
        on[1].wait_recv()
    tok_load.wait()
    cot_load.wait()
    for copy in q_loads:
        copy.wait()
    for copy in o_loads:
        copy.wait()

    def project(n, _):
        cols = aligned(n * 256, 256)
        queries[:, cols] = dot(tok[...], wq[:, cols]).astype(BF16)
        gctx[:, cols] = dot_nt(cot[...], wo[cols, :]).astype(BF16)
        return 0

    lax.fori_loop(0, 2, project, 0)
    for dz in (0, 1, 3, 2):
        for copy in core_opposite[dz]:
            copy.wait_recv()
    keys_values(2)
    flush()

    for h in range(HEADS):
        k_cols = pl.ds(h * HEAD_SIZE, HEAD_SIZE)
        v_cols = pl.ds(FEATURES + h * HEAD_SIZE, HEAD_SIZE)
        scores = dot_nt(queries[:, k_cols], kv[:, k_cols]) * SCALE
        top = jnp.max(scores, axis=-1, keepdims=True)
        weights = jnp.exp(scores - top)
        p = weights / jnp.sum(weights, axis=-1, keepdims=True)
        probs[...] = p
        p_b = p.astype(BF16)
        probs_b[h] = p_b
        grad_probs = dot_nt(gctx[:, k_cols], kv[:, v_cols])
        p = probs[...]
        delta = jnp.sum(grad_probs * p, axis=-1, keepdims=True)
        ds = (p * (grad_probs - delta) * SCALE).astype(BF16)
        dscores[h] = ds
        gkv[:, k_cols] = dot_tn(ds, queries[:, k_cols]).astype(BF16)
        gkv[:, v_cols] = dot_tn(probs_b[h], gctx[:, k_cols]).astype(BF16)

    def memory_terms(dx):
        to_x = x_at(dx)
        rows = aligned(to_x * 256, 256)

        def step(n, _):
            cols = aligned(n * 512, 512)
            mem[to_x, :, cols] = dot_nt(gkv[rows, :], wkv[cols, :]).astype(BF16)
            return 0

        lax.fori_loop(0, 8, step, 0)
        return remote(mem.at[to_x, aligned((1 - c) * 128, 128), :], core_in.at[to_x], CORE)

    def core_piece(dx, dz):
        to_z = lax.rem(z + dz, 4)
        return core_in.at[x_at(dx), aligned(lax.rem(to_z, 2) * 64, 64), side(to_z // 2)]

    def pair_sum(dx, dz, extra=()):
        here = piece(dx, c, dz)
        add_rows(here, [here, core_piece(dx, dz)] + list(extra))
        return here

    GROUP_A, GROUP_B = (2, 3), (1, 0)
    core_2 = memory_terms(2)
    core_1 = memory_terms(1)
    core_2.wait_recv()
    relay_right, relay_left = {}, {}
    for i in range(2):
        relay_right[i] = remote(pair_sum(2, GROUP_A[i]), relay_in.at[0, i], XP)
        relay_left[i] = remote(pair_sum(2, GROUP_B[i]), relay_in.at[1, i], XM)
    core_3 = memory_terms(3)
    core_1.wait_recv()
    to_right, to_left = {}, {}
    for dz in GROUP_B:
        to_right[dz] = remote(pair_sum(1, dz), final_in.at[0, dz], XP)
    core_3.wait_recv()
    for dz in GROUP_A:
        to_left[dz] = remote(pair_sum(3, dz), final_in.at[1, dz], XM)
    core_0 = memory_terms(0)

    def ring_sum(buf, inbox, terms):
        terms(far, 2)
        a_relay = remote(block(buf, far, 2), inbox.at[0], YP)
        terms(near, 2)
        b_relay = remote(block(buf, near, 2), inbox.at[1], YM)
        terms(near, 1)
        b_right = remote(block(buf, near, 1), inbox.at[2], YP)
        terms(far, 3)
        a_left = remote(block(buf, far, 3), inbox.at[3], YM)
        terms(far, 1)
        terms(near, 3)
        terms(far, 0)
        terms(near, 0)
        return a_relay, b_relay, b_right, a_left

    def ring_relay(buf, inbox, copies):
        a_relay, b_relay, b_right, a_left = copies
        a_relay.wait_recv()
        here = block(buf, far, 1)
        add_rows(here, [here, inbox.at[0]])
        a_right = remote(here, inbox.at[4], YP)
        b_relay.wait_recv()
        here = block(buf, near, 3)
        add_rows(here, [here, inbox.at[1]])
        b_left = remote(here, inbox.at[5], YM)
        return b_right, a_left, a_right, b_left

    def ring_far(buf, inbox, z_box, copies):
        b_right, a_left, a_right, b_left = copies
        a_left.wait_recv()
        a_right.wait_recv()
        here = block(buf, far, 0)
        add_rows(here, [here, inbox.at[3], inbox.at[4]])
        return remote(here, z_box, ZFAR)

    def ring_near(buf, inbox, z_box, copies, z_copy, out):
        b_right, a_left, a_right, b_left = copies
        b_right.wait_recv()
        b_left.wait_recv()
        z_copy.wait_recv()
        add_rows(out.at[0], [block(buf, near, 0), inbox.at[2], inbox.at[5], z_box])

    for h in range(HEADS):
        cols = pl.ds(h * HEAD_SIZE, HEAD_SIZE)
        v_cols = pl.ds(FEATURES + h * HEAD_SIZE, HEAD_SIZE)
        ctx[:, cols] = dot(probs_b[h], kv[:, v_cols]).astype(BF16)

    def out_terms(high, dy):
        cols = aligned(high * SIDE + lax.rem(y + dy, 4) * FEATURES, FEATURES)
        tok[:, cols] = dot(ctx[...], wo[:, cols]).astype(BF16)

    att = ring_sum(tok, att_in, out_terms)

    for h in range(HEADS):
        cols = pl.ds(h * HEAD_SIZE, HEAD_SIZE)
        gq[:, cols] = dot(dscores[h], kv[:, cols]).astype(BF16)

    def target_terms(high, dy):
        rows = aligned(high * SIDE + lax.rem(y + dy, 4) * FEATURES, FEATURES)
        cot[:, rows] = dot_nt(gq[...], wq[rows, :]).astype(BF16)

    def x_relay(i):
        relay_right[i].wait_recv()
        dz = GROUP_A[i]
        to_right[dz] = remote(pair_sum(1, dz, [relay_in.at[0, i]]), final_in.at[0, dz], XP)
        relay_left[i].wait_recv()
        dz = GROUP_B[i]
        to_left[dz] = remote(pair_sum(3, dz, [relay_in.at[1, i]]), final_in.at[1, dz], XM)

    x_relay(0)
    att = ring_relay(tok, att_in, att)
    x_relay(1)
    tgt = ring_sum(cot, tgt_in, target_terms)
    core_0.wait_recv()
    att_far = ring_far(tok, att_in, att_z, att)
    tgt = ring_relay(cot, tgt_in, tgt)

    z_copies = {}

    def x_final(dz):
        to_right[dz].wait_recv()
        to_left[dz].wait_recv()
        here = pair_sum(0, dz, [final_in.at[0, dz], final_in.at[1, dz]])
        if dz:
            z_copies[dz] = remote(here, z_in.at[dz - 1], dict(dz=dz))

    x_final(2)
    x_final(1)
    ring_near(tok, att_in, att_z, att, att_far, attended)
    x_final(3)
    x_final(0)
    tgt_far = ring_far(cot, tgt_in, tgt_z, tgt)
    for dz in (2, 1, 3):
        z_copies[dz].wait_recv()
    here = piece(0, c, 0)
    add_rows(here, [here, z_in.at[0], z_in.at[1], z_in.at[2]])

    def y_part(dy):
        return mem.at[
            x, aligned(c * 128 + lax.rem(z, 2) * 64, 64),
            aligned(zh * SIDE + lax.rem(y + dy, 4) * FEATURES, FEATURES),
        ]

    y_copies = [remote(y_part(dy), y_in.at[dy - 1], dict(dy=dy)) for dy in (2, 1, 3)]
    ring_near(cot, tgt_in, tgt_z, tgt, tgt_far, grad_tokens)
    for copy in y_copies:
        copy.wait_recv()
    add_rows(grad_memory, [y_part(0), y_in.at[0], y_in.at[1], y_in.at[2]])
    flush()


def on_device(tokens, cotangent, memory, w_query, w_key, w_value, w_out):
    vmem = pltpu.VMEM
    scratch = [
        vmem((D, 2 * FEATURES), BF16),
        vmem((D, FEATURES), BF16),
        vmem((FEATURES, D), BF16),
        vmem((4, 256, D), BF16),
        vmem((TARGETS, D), BF16),
        vmem((TARGETS, D), BF16),
        vmem((MEMORY, 2 * FEATURES), BF16),
        vmem((MEMORY, 2 * FEATURES), BF16),
        vmem((TARGETS, FEATURES), BF16),
        vmem((TARGETS, FEATURES), BF16),
        vmem((TARGETS, FEATURES), BF16),
        vmem((TARGETS, FEATURES), BF16),
        vmem((TARGETS, MEMORY), F32),
        vmem((HEADS, TARGETS, MEMORY), BF16),
        vmem((HEADS, TARGETS, MEMORY), BF16),
        vmem((4, 128, D), BF16),
        vmem((2, 2, OWN_ROWS, SIDE), BF16),
        vmem((2, 4, OWN_ROWS, SIDE), BF16),
        vmem((3, OWN_ROWS, SIDE), BF16),
        vmem((3, OWN_ROWS, FEATURES), BF16),
        vmem((6, TARGETS, FEATURES), BF16),
        vmem((TARGETS, FEATURES), BF16),
        vmem((6, TARGETS, FEATURES), BF16),
        vmem((TARGETS, FEATURES), BF16),
        pltpu.SemaphoreType.DMA((N_SEMS,)),
        pltpu.SemaphoreType.DMA((N_SEMS,)),
        pltpu.SemaphoreType.DMA((N_LOCAL,)),
    ]
    return pl.pallas_call(
        kernel,
        out_shape=(
            jax.ShapeDtypeStruct(tokens.shape, BF16),
            jax.ShapeDtypeStruct(cotangent.shape, BF16),
            jax.ShapeDtypeStruct(memory.shape, BF16),
        ),
        in_specs=[pl.BlockSpec(memory_space=pl.ANY)] * 7,
        out_specs=(pl.BlockSpec(memory_space=pltpu.VMEM),) * 3,
        scratch_shapes=scratch,
        compiler_params=pltpu.CompilerParams(
            collective_id=0, has_side_effects=True, vmem_limit_bytes=62 * 2**20
        ),
        cost_estimate=pl.CostEstimate(flops=23 * 10**9, bytes_accessed=18 * 2**20, transcendentals=2**19),
    )(tokens, cotangent, memory, w_query, w_key, w_value, w_out)


def solution(mesh):
    placed = (
        P("section", None, "tp"),
        P("section", None, "tp"),
        P("section", "tp"),
        P("section", None, "tp"),
        P("section", None, "tp"),
        P("section", None, "tp"),
        P("section", "tp", None),
    )
    return jax.shard_map(
        on_device,
        mesh=mesh,
        in_specs=placed,
        out_specs=(P("section", None, "tp"), P("section", None, "tp"), P("section", "tp")),
        check_vma=False,
    )
```

time: 1080 us -> 139 us (0.13)
  waiting for transfers between devices: 947 us -> 0 us
  Pallas kernels: 0 us -> 133 us
  matrix products: 74.5 us -> 0 us
  blocking collectives: 33.3 us -> 0 us
  between operations: 14.2 us -> 0.64 us
    reduce_scatter x3 -> x0, waiting for transfers between devices: 814 us -> none  [the longest x1 657 us: on_device(): lax.psum_scatter(block_terms, ('section', 'tp'), scatter_dimension=0, til...]
    pallas_call x0 -> x1, Pallas kernels: none -> 133 us  [on_device(): pl.pallas_call(kernel, out_shape=(jax.ShapeDtypeStruct(tokens.shape, BF16...]
    all_gather x3 -> x0, waiting for transfers between devices: 132 us -> none  [the longest x1 53.9 us: on_device(): lax.all_gather(cotangent[0], 'tp', axis=1, tiled=True)]
    dot_general x13 -> x0, matrix products: 70.8 us -> none  [the longest x1 12.9 us: on_device(): jnp.einsum('smk,tdk->stmd', key_blocks, key_weight_blocks, preferred_elem...]
    all_gather x1 -> x0, blocking collectives: 33.3 us -> none  [on_device(): section_rows = lax.all_gather(memory, 'tp', axis=1, tiled=True)]
  transfers between devices with their start and end apart: 6 -> 0, of which waited for: 6 -> 0; matrix products, arithmetic and copies ran while one was open for 2% -> 0% of each run, Pallas kernels for 0% -> 0%
where the time goes in v1:
time: 139 us; the launch traced here: 138 us
  Pallas kernels  133 us (96%)
  local copies, waits for them, and re-layouts  4.81 us (3%)
    pallas_call x1, Pallas kernels, on_device(): pl.pallas_call(kernel, out_shape=(jax.ShapeDtypeStruct(tokens.shape, BF16...  133 us
    unnamed x3, local copies, waits for them, and re-layouts  4.81 us

profile of v1, /device:TPU:1, one launch (start us, length us, event | category | flops | bytes accessed | tf_op | source)
XLA Modules:
  0.0 138.5 jit_solution(11025115354442489644)
XLA Ops:
  0.6 133.0 %shard_map.94 = (bf16[1,256,512]{2,1,0:T(8,128)(2,1)}, bf16[1,256,512]{2,1,0:T(8,128)(2,1)}, bf16[64,512]{1,0:T(8,128)(2,1)}) custom-call(bf16[1,256,512]{2,1,0:T(8,128)(2,1)} %tokens.1, bf16[1,256,512]{2,1,0:T(8,128)(2,1)} %cotangent.1, bf16[64,512]{1,0:T(8,128)(2,1)} %memory.1, bf16[1,4096,512]{2,1,0:T(8,128)(2,1)} %w_query.1, ...), custom_call_target="tpu_custom_call" | custom-call | flops 23000000512 | bytes 18874368 | tf_op jit(solution)/shard_map/pallas_call | solution.py:468
  133.6 1.7 %copy.13 = bf16[1,256,512]{2,1,0:T(8,128)(2,1)} copy(bf16[1,256,512]{2,1,0:T(8,128)(2,1)} %get-tuple-element.6) | data formatting | bytes 524288
  135.3 1.7 %copy.14 = bf16[1,256,512]{2,1,0:T(8,128)(2,1)} copy(bf16[1,256,512]{2,1,0:T(8,128)(2,1)} %get-tuple-element.7) | data formatting | bytes 524288
  137.0 1.5 %copy.15 = bf16[64,512]{1,0:T(8,128)(2,1)} copy(bf16[64,512]{1,0:T(8,128)(2,1)} %get-tuple-element.8) | data formatting | bytes 131072

commit v2 on v1

v2 whole, which is shorter than its diff:
```python
import functools

import jax
import jax.numpy as jnp
from jax import lax
from jax.experimental import pallas as pl
from jax.experimental.pallas import tpu as pltpu
from jax.sharding import PartitionSpec as P

HEAD_SIZE = 256
HEADS = 2
FEATURES = 512
D = 4096
TARGETS = 256
MEMORY = 1024
OWN_ROWS = 64
SIDE = 2048
SCALE = HEAD_SIZE ** -0.5
BF16 = jnp.bfloat16
F32 = jnp.float32
N_SEMS = 128
N_LOCAL = 48


def dot(a, b):
    return lax.dot_general(a, b, (((1,), (0,)), ((), ())), preferred_element_type=F32)


def dot_nt(a, b):
    return lax.dot_general(a, b, (((1,), (1,)), ((), ())), preferred_element_type=F32)


def dot_tn(a, b):
    return lax.dot_general(a, b, (((0,), (0,)), ((), ())), preferred_element_type=F32)


def aligned(start, size):
    return pl.ds(pl.multiple_of(start, size), size)


def add_rows(dst, srcs):
    rows = dst.shape[0]

    def step(i, _):
        part = aligned(i * 16, 16)
        total = srcs[0][part, :].astype(F32)
        for src in srcs[1:]:
            total = total + src[part, :].astype(F32)
        dst[part, :] = total.astype(dst.dtype)
        return 0

    lax.fori_loop(0, rows // 16, step, 0)


def kernel(
    tokens, cotangent, memory, w_query, w_key, w_value, w_out,
    attended, grad_tokens, grad_memory,
    wkv, wq, wo, mem, tok, cot, kv, gkv, queries_acc, gctx_acc, queries, gctx, ctx, gq, probs, probs_b, dscores,
    core_in, opposite_in, relay_in, final_in, z_in, y_in, att_in, att_z, tgt_in, tgt_z,
    send_sem, recv_sem, local_sem,
):
    section = lax.axis_index("section")
    tp = lax.axis_index("tp")
    c = lax.rem(section, 2)
    x = lax.rem(section // 2, 4)
    y = tp // 2
    zh = lax.rem(tp, 2)
    z = zh * 2 + section // 8

    def device(dx=0, dy=0, dz=0, dc=0):
        to_x, to_y, to_z = lax.rem(x + dx, 4), lax.rem(y + dy, 4), lax.rem(z + dz, 4)
        to_c = lax.rem(c + dc, 2)
        return ((lax.rem(to_z, 2) * 4 + to_x) * 2 + to_c, to_y * 2 + to_z // 2)

    counter = [0, 0]
    sends = []

    def remote(src, dst, where):
        i = counter[0]
        counter[0] += 1
        copy = pltpu.make_async_remote_copy(
            src_ref=src, dst_ref=dst, send_sem=send_sem.at[i], recv_sem=recv_sem.at[i],
            device_id=device(**where), device_id_type=pl.DeviceIdType.MESH,
        )
        copy.start()
        sends.append(copy)
        return copy

    def local(src, dst):
        i = counter[1]
        counter[1] += 1
        copy = pltpu.make_async_copy(src, dst, local_sem.at[i])
        copy.start()
        return copy

    def flush():
        for copy in sends:
            copy.wait_send()
        sends.clear()

    XP, XM, YP, YM = dict(dx=1), dict(dx=3), dict(dy=1), dict(dy=3)
    CORE, ZFAR = dict(dc=1), dict(dz=2)

    def x_at(dx):
        return lax.rem(x + dx, 4)

    def side(high):
        return aligned(high * SIDE, SIDE)

    def piece(dx, core, dz, half=None):
        to_z = lax.rem(z + dz, 4)
        row = core * 128 + lax.rem(to_z, 2) * 64
        rows = aligned(row, 64) if half is None else aligned(row + half * 32, 32)
        return mem.at[x_at(dx), rows, side(to_z // 2)]

    def block(buf, high, dy):
        return buf.at[:, aligned(high * SIDE + lax.rem(y + dy, 4) * FEATURES, FEATURES)]

    own_mem = mem.at[x, aligned(c * 128 + lax.rem(z, 2) * 64, 64), aligned(zh * SIDE + y * FEATURES, FEATURES)]
    near, far = zh, 1 - zh

    mem_load = local(memory, own_mem)
    tok_load = local(tokens.at[0], block(tok, near, 0))
    cot_load = local(cotangent.at[0], block(cot, near, 0))
    barrier = pltpu.get_barrier_semaphore()
    peers = [XP, XM, YP, YM, dict(dy=2), dict(dz=1), dict(dz=3), ZFAR, CORE]
    for where in peers:
        pl.semaphore_signal(barrier, inc=1, device_id=device(**where), device_id_type=pl.DeviceIdType.MESH)
    pl.semaphore_wait(barrier, len(peers))

    mem_y = {dy: remote(memory, own_mem, dict(dy=dy)) for dy in (1, 3, 2)}
    right, left, core_own, mem_z = {}, {}, {}, {}
    right[0] = [remote(memory, own_mem, XP)]
    left[0] = [remote(memory, own_mem, XM)]
    mem_z[1] = [remote(memory, own_mem, dict(dz=1))]
    mem_z[3] = [remote(memory, own_mem, dict(dz=3))]
    tok_z = remote(tokens.at[0], block(tok, near, 0), ZFAR)
    mem_load.wait()
    for dy in (1, 3, 2):
        mem_y[dy].wait_recv()
        here = mem.at[
            x, aligned(c * 128 + lax.rem(z, 2) * 64, 64), aligned(zh * SIDE + lax.rem(y + 4 - dy, 4) * FEATURES, FEATURES)
        ]
        right[0].append(remote(here, here, XP))
        left[0].append(remote(here, here, XM))
        mem_z[1].append(remote(here, here, dict(dz=1)))
        mem_z[3].append(remote(here, here, dict(dz=3)))
    own = piece(0, c, 0)
    core_right, core_left, core_opposite = {}, {}, {}
    on_right, on_left = {}, {}

    def spread(dz):
        here = piece(0, c, dz)
        right[dz] = [remote(here, here, XP)]
        left[dz] = [remote(here, here, XM)]
        core_own[dz] = remote(here, here, CORE)

    def spread_targets():
        t, g = tokens.at[0], cotangent.at[0]
        t_dst, g_dst = block(tok, near, 0), block(cot, near, 0)
        t_right = remote(t, t_dst, YP)
        g_left = remote(g, g_dst, YM)
        g_right = remote(g, g_dst, YP)
        t_left = remote(t, t_dst, YM)
        return t_right, g_left, g_right, t_left

    def spread_far(buf):
        here = block(buf, far, 0)
        return remote(here, here, YP), remote(here, here, YM)

    def arrive_x(dz):
        for copy in right[dz]:
            copy.wait_recv()
        if dz in (0, 2):
            on_right[dz] = remote(piece(3, c, dz, 0), piece(3, c, dz, 0), XP)
        core_left[dz] = remote(piece(3, c, dz), piece(3, c, dz), CORE)
        for copy in left[dz]:
            copy.wait_recv()
        if dz in (0, 2):
            on_left[dz] = remote(piece(1, c, dz, 1), piece(1, c, dz, 1), XM)
        core_right[dz] = remote(piece(1, c, dz), piece(1, c, dz), CORE)

    def arrive_opposite(dz):
        on_right[dz].wait_recv()
        a = remote(piece(2, c, dz, 0), piece(2, c, dz, 0), CORE)
        on_left[dz].wait_recv()
        b = remote(piece(2, c, dz, 1), piece(2, c, dz, 1), CORE)
        core_opposite[dz] = (a, b)

    def arrive_opposite_z(dz):
        opposite_z[4 - dz].wait_recv()
        core_opposite[dz] = (remote(piece(2, c, dz), piece(2, c, dz), CORE),)

    def forward_targets(high, ring):
        t_right, g_left, g_right, t_left = ring
        t_right.wait_recv()
        t_on = remote(block(tok, high, 3), block(tok, high, 3), YP)
        g_left.wait_recv()
        g_on = remote(block(cot, high, 1), block(cot, high, 1), YM)
        return t_on, g_on

    def keys_values(dx):
        to_x = x_at(dx)
        rows = aligned(to_x * 256, 256)

        def step(n, _):
            cols = aligned(n * 256, 256)
            kv[rows, cols] = dot(mem[to_x], wkv[:, cols]).astype(BF16)
            return 0

        lax.fori_loop(0, 4, step, 0)

    core_own[0] = remote(own, own, CORE)
    near_ring = spread_targets()
    kv_loads, q_loads, o_loads = [], [], []
    for high in range(2):
        for row in range(4):
            src = pl.ds((row * 2 + high) * FEATURES, FEATURES)
            dst = pl.ds(high * SIDE + row * FEATURES, FEATURES)
            kv_loads.append(local(w_key.at[0, src, :], wkv.at[dst, pl.ds(0, FEATURES)]))
            kv_loads.append(local(w_value.at[0, src, :], wkv.at[dst, pl.ds(FEATURES, FEATURES)]))
    tok_z.wait_recv()
    far_tok = spread_far(tok)
    arrive_x(0)
    for dz in (1, 3):
        for copy in mem_z[4 - dz]:
            copy.wait_recv()
        spread(dz)
    mem_z[2] = remote(own, own, ZFAR)
    cot_z = remote(cotangent.at[0], block(cot, near, 0), ZFAR)
    for high in range(2):
        for row in range(4):
            src = pl.ds((row * 2 + high) * FEATURES, FEATURES)
            dst = pl.ds(high * SIDE + row * FEATURES, FEATURES)
            q_loads.append(local(w_query.at[0, src, :], wq.at[dst, :]))
            o_loads.append(local(w_out.at[0, :, src], wo.at[:, dst]))

    near_on = forward_targets(near, near_ring)
    arrive_opposite(0)
    opposite_z = {dz: remote(piece(2, c, 0), piece(2, c, 0), dict(dz=dz)) for dz in (1, 3)}
    mem_z[2].wait_recv()
    spread(2)
    cot_z.wait_recv()
    far_cot = spread_far(cot)
    for copy in kv_loads:
        copy.wait()
    for dz in (0, 1, 3, 2):
        core_own[dz].wait_recv()
    keys_values(0)
    arrive_x(1)
    arrive_x(3)
    far_tok[0].wait_recv()
    far_t_on = remote(block(tok, far, 3), block(tok, far, 3), YP)

    def complete(ring, on):
        t_right, g_left, g_right, t_left = ring
        g_right.wait_recv()
        t_left.wait_recv()
        on[0].wait_recv()
        on[1].wait_recv()

    complete(near_ring, near_on)
    tok_load.wait()
    cot_load.wait()
    for copy in q_loads:
        copy.wait()
    for copy in o_loads:
        copy.wait()

    def project_near(n, _):
        cols = aligned(n * 256, 256)
        queries_acc[:, cols] = dot(tok[:, side(near)], wq[side(near), cols])
        gctx_acc[:, cols] = dot_nt(cot[:, side(near)], wo[cols, side(near)])
        return 0

    lax.fori_loop(0, 2, project_near, 0)
    arrive_opposite_z(1)
    arrive_opposite_z(3)
    arrive_x(2)
    far_cot[1].wait_recv()
    far_g_on = remote(block(cot, far, 1), block(cot, far, 1), YM)
    far_on = (far_t_on, far_g_on)
    far_ring = (far_tok[0], far_cot[1], far_cot[0], far_tok[1])
    arrive_opposite(2)
    for dz in (0, 1, 3, 2):
        core_right[dz].wait_recv()
    keys_values(1)
    for dz in (0, 1, 3, 2):
        core_left[dz].wait_recv()
    keys_values(3)
    for dz in (0, 1, 3, 2):
        for copy in core_opposite[dz]:
            copy.wait_recv()
    keys_values(2)
    complete(far_ring, far_on)

    def project_far(n, _):
        cols = aligned(n * 256, 256)
        queries[:, cols] = (queries_acc[:, cols] + dot(tok[:, side(far)], wq[side(far), cols])).astype(BF16)
        gctx[:, cols] = (gctx_acc[:, cols] + dot_nt(cot[:, side(far)], wo[cols, side(far)])).astype(BF16)
        return 0

    lax.fori_loop(0, 2, project_far, 0)
    flush()

    for h in range(HEADS):
        k_cols = pl.ds(h * HEAD_SIZE, HEAD_SIZE)
        v_cols = pl.ds(FEATURES + h * HEAD_SIZE, HEAD_SIZE)
        scores = dot_nt(queries[:, k_cols], kv[:, k_cols]) * SCALE
        top = jnp.max(scores, axis=-1, keepdims=True)
        weights = jnp.exp(scores - top)
        p = weights / jnp.sum(weights, axis=-1, keepdims=True)
        probs[...] = p
        p_b = p.astype(BF16)
        probs_b[h] = p_b
        grad_probs = dot_nt(gctx[:, k_cols], kv[:, v_cols])
        p = probs[...]
        delta = jnp.sum(grad_probs * p, axis=-1, keepdims=True)
        ds = (p * (grad_probs - delta) * SCALE).astype(BF16)
        dscores[h] = ds
        gkv[:, k_cols] = dot_tn(ds, queries[:, k_cols]).astype(BF16)
        gkv[:, v_cols] = dot_tn(probs_b[h], gctx[:, k_cols]).astype(BF16)

    def memory_terms(dx, high):
        to_x = x_at(dx)
        rows = aligned(to_x * 256, 256)

        def step(n, _):
            cols = aligned(high * SIDE + n * 512, 512)
            mem[to_x, :, cols] = dot_nt(gkv[rows, :], wkv[cols, :]).astype(BF16)
            return 0

        lax.fori_loop(0, 4, step, 0)
        return remote(
            mem.at[to_x, aligned((1 - c) * 128, 128), side(high)], core_in.at[to_x, :, side(high)], CORE
        )

    zl = lax.rem(z, 2)

    def part(dx, high, low):
        return mem.at[x_at(dx), aligned(c * 128 + low * 64, 64), side(high)]

    def pair_sum(dx, high, low, extra=()):
        here = part(dx, high, low)
        other = core_in.at[x_at(dx), aligned(low * 64, 64), side(high)]
        add_rows(here, [here, other] + list(extra))
        return here

    def far_relay(buf, inbox):
        return remote(block(buf, far, 2), inbox.at[0], YP)

    def near_relay(buf, inbox):
        return remote(block(buf, near, 2), inbox.at[1], YM)

    def far_on_left(buf, inbox, terms):
        terms(far, 3)
        return remote(block(buf, far, 3), inbox.at[3], YM)

    def near_on_right(buf, inbox, terms):
        terms(near, 1)
        return remote(block(buf, near, 1), inbox.at[2], YP)

    def far_on_right(buf, inbox, a_relay):
        a_relay.wait_recv()
        here = block(buf, far, 1)
        add_rows(here, [here, inbox.at[0]])
        return remote(here, inbox.at[4], YP)

    def near_on_left(buf, inbox, b_relay):
        b_relay.wait_recv()
        here = block(buf, near, 3)
        add_rows(here, [here, inbox.at[1]])
        return remote(here, inbox.at[5], YM)

    def ring_far(buf, inbox, z_box, a_left, a_right):
        a_left.wait_recv()
        a_right.wait_recv()
        here = block(buf, far, 0)
        add_rows(here, [here, inbox.at[3], inbox.at[4]])
        return remote(here, z_box, ZFAR)

    def ring_near(buf, inbox, z_box, b_right, b_left, z_copy, out):
        b_right.wait_recv()
        b_left.wait_recv()
        z_copy.wait_recv()
        add_rows(out.at[0], [block(buf, near, 0), inbox.at[2], inbox.at[5], z_box])

    def out_terms(high, dy):
        cols = aligned(high * SIDE + lax.rem(y + dy, 4) * FEATURES, FEATURES)
        tok[:, cols] = dot(ctx[...], wo[:, cols]).astype(BF16)

    def target_terms(high, dy):
        rows = aligned(high * SIDE + lax.rem(y + dy, 4) * FEATURES, FEATURES)
        cot[:, rows] = dot_nt(gq[...], wq[rows, :]).astype(BF16)

    lows = (zl, 1 - zl)
    far_lows, near_lows = lows, lows[::-1]

    def x_final_far(i):
        far_left[i].wait_recv()
        far_right[i].wait_recv()
        here = pair_sum(0, far, far_lows[i], [final_in.at[0, i], final_in.at[1, i]])
        if i == 0:
            return remote(here, z_in.at[0], ZFAR)
        return remote(here, z_in.at[1], dict(dz=3 - 2 * zl))

    def x_final_near(i):
        near_right[i].wait_recv()
        near_left[i].wait_recv()
        here = pair_sum(0, near, near_lows[i], [final_in.at[0, 2 + i], final_in.at[1, 2 + i]])
        if i == 0:
            return remote(here, z_in.at[2], dict(dz=1 + 2 * zl))
        return here

    core_2f = memory_terms(2, far)
    core_3f = memory_terms(3, far)
    for h in range(HEADS):
        cols = pl.ds(h * HEAD_SIZE, HEAD_SIZE)
        v_cols = pl.ds(FEATURES + h * HEAD_SIZE, HEAD_SIZE)
        ctx[:, cols] = dot(probs_b[h], kv[:, v_cols]).astype(BF16)
    out_terms(far, 2)
    att_far_relay = far_relay(tok, att_in)
    att_far_left = far_on_left(tok, att_in, out_terms)
    core_2f.wait_recv()
    opposite_far = remote(pair_sum(2, far, 1 - zl), opposite_in.at[1], dict(dz=3 - 2 * zl))
    relay_right = remote(pair_sum(2, far, zl), relay_in.at[0], XP)
    core_2n = memory_terms(2, near)
    core_3f.wait_recv()
    far_left = [remote(pair_sum(3, far, zl), final_in.at[1, 0], XM)]
    for h in range(HEADS):
        cols = pl.ds(h * HEAD_SIZE, HEAD_SIZE)
        gq[:, cols] = dot(dscores[h], kv[:, cols]).astype(BF16)
    out_terms(far, 1)
    target_terms(far, 2)
    core_1f = memory_terms(1, far)
    core_2n.wait_recv()
    opposite_near = remote(pair_sum(2, near, 1 - zl), opposite_in.at[0], dict(dz=1 + 2 * zl))
    target_terms(far, 1)
    far_left.append(remote(pair_sum(3, far, 1 - zl), final_in.at[1, 1], XM))
    core_1n = memory_terms(1, near)
    out_terms(near, 2)
    att_far_right = far_on_right(tok, att_in, att_far_relay)
    tgt_far_relay = far_relay(cot, tgt_in)
    tgt_far_left = far_on_left(cot, tgt_in, target_terms)
    core_1f.wait_recv()
    relay_right.wait_recv()
    far_right = [remote(pair_sum(1, far, zl, [relay_in.at[0]]), final_in.at[0, 0], XP)]
    opposite_near.wait_recv()
    opposite_far.wait_recv()
    relay_left = remote(
        pair_sum(2, near, zl, [opposite_in.at[0], opposite_in.at[1]]), relay_in.at[1], XM
    )
    att_near_relay = near_relay(tok, att_in)
    core_0f = memory_terms(0, far)
    far_right.append(remote(pair_sum(1, far, 1 - zl), final_in.at[0, 1], XP))
    out_terms(far, 0)
    core_3n = memory_terms(3, near)
    target_terms(near, 2)
    core_0f.wait_recv()
    att_far = ring_far(tok, att_in, att_z, att_far_left, att_far_right)
    z_far0 = x_final_far(0)
    core_1n.wait_recv()
    near_right = [remote(pair_sum(1, near, 1 - zl), final_in.at[0, 2], XP)]
    core_3n.wait_recv()
    near_left = [remote(pair_sum(3, near, 1 - zl), final_in.at[1, 2], XM)]
    tgt_near_relay = near_relay(cot, tgt_in)
    att_near_right = near_on_right(tok, att_in, out_terms)
    target_terms(far, 0)
    out_terms(near, 3)
    target_terms(near, 3)
    tgt_far_right = far_on_right(cot, tgt_in, tgt_far_relay)
    z_far1 = x_final_far(1)
    near_right.append(remote(pair_sum(1, near, zl), final_in.at[0, 3], XP))
    relay_left.wait_recv()
    near_left.append(remote(pair_sum(3, near, zl, [relay_in.at[1]]), final_in.at[1, 3], XM))
    tgt_near_right = near_on_right(cot, tgt_in, target_terms)
    att_near_left = near_on_left(tok, att_in, att_near_relay)
    core_0n = memory_terms(0, near)
    out_terms(near, 0)
    target_terms(near, 0)
    core_0n.wait_recv()
    tgt_near_left = near_on_left(cot, tgt_in, tgt_near_relay)
    z_near0 = x_final_near(0)
    tgt_far = ring_far(cot, tgt_in, tgt_z, tgt_far_left, tgt_far_right)
    here = x_final_near(1)
    for copy in (z_far0, z_near0, z_far1):
        copy.wait_recv()
    add_rows(here, [here, z_in.at[0], z_in.at[1], z_in.at[2]])

    def y_part(dy):
        return mem.at[
            x, aligned(c * 128 + zl * 64, 64), aligned(zh * SIDE + lax.rem(y + dy, 4) * FEATURES, FEATURES)
        ]

    y_copies = [remote(y_part(dy), y_in.at[dy - 1], dict(dy=dy)) for dy in (2, 1, 3)]
    ring_near(tok, att_in, att_z, att_near_right, att_near_left, att_far, attended)
    ring_near(cot, tgt_in, tgt_z, tgt_near_right, tgt_near_left, tgt_far, grad_tokens)
    for copy in y_copies:
        copy.wait_recv()
    add_rows(grad_memory, [y_part(0), y_in.at[0], y_in.at[1], y_in.at[2]])
    flush()


def hand_over(a_in, b_in, c_in, a_out, b_out, c_out):
    a_out[...] = a_in[...]
    b_out[...] = b_in[...]
    c_out[...] = c_in[...]


def on_device(tokens, cotangent, memory, w_query, w_key, w_value, w_out):
    vmem = pltpu.VMEM
    scratch = [
        vmem((D, 2 * FEATURES), BF16),
        vmem((D, FEATURES), BF16),
        vmem((FEATURES, D), BF16),
        vmem((4, 256, D), BF16),
        vmem((TARGETS, D), BF16),
        vmem((TARGETS, D), BF16),
        vmem((MEMORY, 2 * FEATURES), BF16),
        vmem((MEMORY, 2 * FEATURES), BF16),
        vmem((TARGETS, FEATURES), F32),
        vmem((TARGETS, FEATURES), F32),
        vmem((TARGETS, FEATURES), BF16),
        vmem((TARGETS, FEATURES), BF16),
        vmem((TARGETS, FEATURES), BF16),
        vmem((TARGETS, FEATURES), BF16),
        vmem((TARGETS, MEMORY), F32),
        vmem((HEADS, TARGETS, MEMORY), BF16),
        vmem((HEADS, TARGETS, MEMORY), BF16),
        vmem((4, 128, D), BF16),
        vmem((2, OWN_ROWS, SIDE), BF16),
        vmem((2, OWN_ROWS, SIDE), BF16),
        vmem((2, 4, OWN_ROWS, SIDE), BF16),
        vmem((3, OWN_ROWS, SIDE), BF16),
        vmem((3, OWN_ROWS, FEATURES), BF16),
        vmem((6, TARGETS, FEATURES), BF16),
        vmem((TARGETS, FEATURES), BF16),
        vmem((6, TARGETS, FEATURES), BF16),
        vmem((TARGETS, FEATURES), BF16),
        pltpu.SemaphoreType.DMA((N_SEMS,)),
        pltpu.SemaphoreType.DMA((N_SEMS,)),
        pltpu.SemaphoreType.DMA((N_LOCAL,)),
    ]
    results = pl.pallas_call(
        kernel,
        out_shape=(
            jax.ShapeDtypeStruct(tokens.shape, BF16),
            jax.ShapeDtypeStruct(cotangent.shape, BF16),
            jax.ShapeDtypeStruct(memory.shape, BF16),
        ),
        in_specs=[pl.BlockSpec(memory_space=pl.ANY)] * 7,
        out_specs=(pl.BlockSpec(memory_space=pltpu.VMEM),) * 3,
        scratch_shapes=scratch,
        compiler_params=pltpu.CompilerParams(
            collective_id=0, has_side_effects=True, vmem_limit_bytes=62 * 2**20
        ),
        cost_estimate=pl.CostEstimate(flops=23 * 10**9, bytes_accessed=18 * 2**20, transcendentals=2**19),
    )(tokens, cotangent, memory, w_query, w_key, w_value, w_out)
    return pl.pallas_call(
        hand_over,
        out_shape=tuple(jax.ShapeDtypeStruct(r.shape, r.dtype) for r in results),
        in_specs=[pl.BlockSpec(memory_space=pltpu.VMEM)] * 3,
        out_specs=(pl.BlockSpec(memory_space=pltpu.VMEM),) * 3,
    )(*results)


def solution(mesh):
    placed = (
        P("section", None, "tp"),
        P("section", None, "tp"),
        P("section", "tp"),
        P("section", None, "tp"),
        P("section", None, "tp"),
        P("section", None, "tp"),
        P("section", "tp", None),
    )
    return jax.shard_map(
        on_device,
        mesh=mesh,
        in_specs=placed,
        out_specs=(P("section", None, "tp"), P("section", None, "tp"), P("section", "tp")),
        check_vma=False,
    )
```

time: 139 us -> 111 us (0.80)
  Pallas kernels: 133 us -> 110 us
  local copies, waits for them, and re-layouts: 4.81 us -> 0 us
    pallas_call x1, Pallas kernels: 133 us -> 108 us  [on_device(): pl.pallas_call(kernel, out_shape=(jax.ShapeDtypeStruct(tokens.shape, BF16...]
    unnamed x3 -> x0, local copies, waits for them, and re-layouts: 4.81 us -> none
    pallas_call x0 -> x1, Pallas kernels: none -> 1.85 us  [on_device(): pl.pallas_call(hand_over, out_shape=tuple((jax.ShapeDtypeStruct(r.shape,...]
where the time goes in v2:
time: 111 us; the launch traced here: 110 us
  Pallas kernels  110 us (99%)
    pallas_call x1, Pallas kernels, on_device(): pl.pallas_call(kernel, out_shape=(jax.ShapeDtypeStruct(tokens.shape, BF16...  108 us

profile of v2, /device:TPU:1, one launch (start us, length us, event | category | flops | bytes accessed | tf_op | source)
XLA Modules:
  0.0 110.4 jit_solution(10785428136634261547)
XLA Ops:
  0.6 107.9 %shard_map.94 = (bf16[1,256,512]{2,1,0:T(8,128)(2,1)}, bf16[1,256,512]{2,1,0:T(8,128)(2,1)}, bf16[64,512]{1,0:T(8,128)(2,1)}) custom-call(bf16[1,256,512]{2,1,0:T(8,128)(2,1)} %tokens.1, bf16[1,256,512]{2,1,0:T(8,128)(2,1)} %cotangent.1, bf16[64,512]{1,0:T(8,128)(2,1)} %memory.1, bf16[1,4096,512]{2,1,0:T(8,128)(2,1)} %w_query.1, ...), custom_call_target="tpu_custom_call" | custom-call | flops 23000000512 | bytes 18874368 | tf_op jit(solution)/shard_map/pallas_call | solution.py:544
  108.5 1.9 %shard_map.95 = (bf16[1,256,512]{2,1,0:T(8,128)(2,1)}, bf16[1,256,512]{2,1,0:T(8,128)(2,1)}, bf16[64,512]{1,0:T(8,128)(2,1)}) custom-call(bf16[1,256,512]{2,1,0:T(8,128)(2,1)} %get-tuple-element.6.a_in, bf16[1,256,512]{2,1,0:T(8,128)(2,1)} %get-tuple-element.7.b_in, bf16[64,512]{1,0:T(8,128)(2,1)} %get-tuple-element.8.c_in), custom_call_target="tpu_custom_call" | custom-call | tf_op jit(solution)/shard_map/pallas_call | solution.py:559

commit v3 on v2

--- a/solution.py
+++ b/solution.py
@@ -204,11 +204,11 @@
         rows = aligned(to_x * 256, 256)
 
         def step(n, _):
-            cols = aligned(n * 256, 256)
+            cols = aligned(n * 512, 512)
             kv[rows, cols] = dot(mem[to_x], wkv[:, cols]).astype(BF16)
             return 0
 
-        lax.fori_loop(0, 4, step, 0)
+        lax.fori_loop(0, 2, step, 0)
 
     core_own[0] = remote(own, own, CORE)
     near_ring = spread_targets()
@@ -267,13 +267,11 @@
     for copy in o_loads:
         copy.wait()
 
-    def project_near(n, _):
-        cols = aligned(n * 256, 256)
-        queries_acc[:, cols] = dot(tok[:, side(near)], wq[side(near), cols])
-        gctx_acc[:, cols] = dot_nt(cot[:, side(near)], wo[cols, side(near)])
-        return 0
-
-    lax.fori_loop(0, 2, project_near, 0)
+    def project_near():
+        queries_acc[...] = dot(tok[:, side(near)], wq[side(near), :])
+        gctx_acc[...] = dot_nt(cot[:, side(near)], wo[:, side(near)])
+
+    project_near()
     arrive_opposite_z(1)
     arrive_opposite_z(3)
     arrive_x(2)
@@ -281,10 +279,10 @@
     far_g_on = remote(block(cot, far, 1), block(cot, far, 1), YM)
     far_on = (far_t_on, far_g_on)
     far_ring = (far_tok[0], far_cot[1], far_cot[0], far_tok[1])
-    arrive_opposite(2)
     for dz in (0, 1, 3, 2):
         core_right[dz].wait_recv()
     keys_values(1)
+    arrive_opposite(2)
     for dz in (0, 1, 3, 2):
         core_left[dz].wait_recv()
     keys_values(3)
@@ -294,13 +292,11 @@
     keys_values(2)
     complete(far_ring, far_on)
 
-    def project_far(n, _):
-        cols = aligned(n * 256, 256)
-        queries[:, cols] = (queries_acc[:, cols] + dot(tok[:, side(far)], wq[side(far), cols])).astype(BF16)
-        gctx[:, cols] = (gctx_acc[:, cols] + dot_nt(cot[:, side(far)], wo[cols, side(far)])).astype(BF16)
-        return 0
-
-    lax.fori_loop(0, 2, project_far, 0)
+    def project_far():
+        queries[...] = (queries_acc[...] + dot(tok[:, side(far)], wq[side(far), :])).astype(BF16)
+        gctx[...] = (gctx_acc[...] + dot_nt(cot[:, side(far)], wo[:, side(far)])).astype(BF16)
+
+    project_far()
     flush()
 
     for h in range(HEADS):

time: 111 us -> 108 us (0.973)
  Pallas kernels: 110 us -> 107 us
    pallas_call x1, Pallas kernels: 108 us -> 105 us  [on_device(): pl.pallas_call(kernel, out_shape=(jax.ShapeDtypeStruct(tokens.shape, BF16...]
where the time goes in v3:
time: 108 us; the launch traced here: 107 us
  Pallas kernels  107 us (99%)
    pallas_call x1, Pallas kernels, on_device(): pl.pallas_call(kernel, out_shape=(jax.ShapeDtypeStruct(tokens.shape, BF16...  105 us

profile of v3, /device:TPU:1, one launch (start us, length us, event | category | flops | bytes accessed | tf_op | source)
XLA Modules:
  0.0 107.4 jit_solution(2813788965786670790)
XLA Ops:
  0.6 104.9 %shard_map.94 = (bf16[1,256,512]{2,1,0:T(8,128)(2,1)}, bf16[1,256,512]{2,1,0:T(8,128)(2,1)}, bf16[64,512]{1,0:T(8,128)(2,1)}) custom-call(bf16[1,256,512]{2,1,0:T(8,128)(2,1)} %tokens.1, bf16[1,256,512]{2,1,0:T(8,128)(2,1)} %cotangent.1, bf16[64,512]{1,0:T(8,128)(2,1)} %memory.1, bf16[1,4096,512]{2,1,0:T(8,128)(2,1)} %w_query.1, ...), custom_call_target="tpu_custom_call" | custom-call | flops 23000000512 | bytes 18874368 | tf_op jit(solution)/shard_map/pallas_call | solution.py:540
  105.6 1.9 %shard_map.95 = (bf16[1,256,512]{2,1,0:T(8,128)(2,1)}, bf16[1,256,512]{2,1,0:T(8,128)(2,1)}, bf16[64,512]{1,0:T(8,128)(2,1)}) custom-call(bf16[1,256,512]{2,1,0:T(8,128)(2,1)} %get-tuple-element.6.a_in, bf16[1,256,512]{2,1,0:T(8,128)(2,1)} %get-tuple-element.7.b_in, bf16[64,512]{1,0:T(8,128)(2,1)} %get-tuple-element.8.c_in), custom_call_target="tpu_custom_call" | custom-call | tf_op jit(solution)/shard_map/pallas_call | solution.py:555

commit v4 on v3

--- a/solution.py
+++ b/solution.py
@@ -171,12 +171,12 @@
     def arrive_x(dz):
         for copy in right[dz]:
             copy.wait_recv()
-        if dz in (0, 2):
+        if dz == 0:
             on_right[dz] = remote(piece(3, c, dz, 0), piece(3, c, dz, 0), XP)
         core_left[dz] = remote(piece(3, c, dz), piece(3, c, dz), CORE)
         for copy in left[dz]:
             copy.wait_recv()
-        if dz in (0, 2):
+        if dz == 0:
             on_left[dz] = remote(piece(1, c, dz, 1), piece(1, c, dz, 1), XM)
         core_right[dz] = remote(piece(1, c, dz), piece(1, c, dz), CORE)
 
@@ -237,7 +237,7 @@
 
     near_on = forward_targets(near, near_ring)
     arrive_opposite(0)
-    opposite_z = {dz: remote(piece(2, c, 0), piece(2, c, 0), dict(dz=dz)) for dz in (1, 3)}
+    opposite_z = {dz: remote(piece(2, c, 0), piece(2, c, 0), dict(dz=dz)) for dz in (1, 3, 2)}
     mem_z[2].wait_recv()
     spread(2)
     cot_z.wait_recv()
@@ -279,10 +279,10 @@
     far_g_on = remote(block(cot, far, 1), block(cot, far, 1), YM)
     far_on = (far_t_on, far_g_on)
     far_ring = (far_tok[0], far_cot[1], far_cot[0], far_tok[1])
+    arrive_opposite_z(2)
     for dz in (0, 1, 3, 2):
         core_right[dz].wait_recv()
     keys_values(1)
-    arrive_opposite(2)
     for dz in (0, 1, 3, 2):
         core_left[dz].wait_recv()
     keys_values(3)
@@ -408,7 +408,10 @@
             return remote(here, z_in.at[2], dict(dz=1 + 2 * zl))
         return here
 
-    core_2f = memory_terms(2, far)
+    def half(dx, i):
+        return mem.at[x_at(dx), aligned(c * 128 + zl * 64 + i * 32, 32), side(near)]
+
+    core_1f = memory_terms(1, far)
     core_3f = memory_terms(3, far)
     for h in range(HEADS):
         cols = pl.ds(h * HEAD_SIZE, HEAD_SIZE)
@@ -417,66 +420,70 @@
     out_terms(far, 2)
     att_far_relay = far_relay(tok, att_in)
     att_far_left = far_on_left(tok, att_in, out_terms)
-    core_2f.wait_recv()
-    opposite_far = remote(pair_sum(2, far, 1 - zl), opposite_in.at[1], dict(dz=3 - 2 * zl))
-    relay_right = remote(pair_sum(2, far, zl), relay_in.at[0], XP)
-    core_2n = memory_terms(2, near)
+    core_1f.wait_recv()
+    far_right = [remote(pair_sum(1, far, zl), final_in.at[0, 0], XP)]
     core_3f.wait_recv()
     far_left = [remote(pair_sum(3, far, zl), final_in.at[1, 0], XM)]
+    core_2f = memory_terms(2, far)
+    core_2n = memory_terms(2, near)
     for h in range(HEADS):
         cols = pl.ds(h * HEAD_SIZE, HEAD_SIZE)
         gq[:, cols] = dot(dscores[h], kv[:, cols]).astype(BF16)
-    out_terms(far, 1)
-    target_terms(far, 2)
-    core_1f = memory_terms(1, far)
+    core_2f.wait_recv()
+    opposite_other = remote(pair_sum(2, far, 1 - zl), opposite_in.at[1], dict(dz=3 - 2 * zl))
+    opposite_same = remote(pair_sum(2, far, zl), opposite_in.at[2], ZFAR)
     core_2n.wait_recv()
     opposite_near = remote(pair_sum(2, near, 1 - zl), opposite_in.at[0], dict(dz=1 + 2 * zl))
+    far_right.append(remote(pair_sum(1, far, 1 - zl), final_in.at[0, 1], XP))
+    far_left.append(remote(pair_sum(3, far, 1 - zl), final_in.at[1, 1], XM))
+    out_terms(far, 1)
+    core_0f = memory_terms(0, far)
+    target_terms(far, 2)
     target_terms(far, 1)
-    far_left.append(remote(pair_sum(3, far, 1 - zl), final_in.at[1, 1], XM))
-    core_1n = memory_terms(1, near)
     out_terms(near, 2)
     att_far_right = far_on_right(tok, att_in, att_far_relay)
     tgt_far_relay = far_relay(cot, tgt_in)
     tgt_far_left = far_on_left(cot, tgt_in, target_terms)
-    core_1f.wait_recv()
-    relay_right.wait_recv()
-    far_right = [remote(pair_sum(1, far, zl, [relay_in.at[0]]), final_in.at[0, 0], XP)]
-    opposite_near.wait_recv()
-    opposite_far.wait_recv()
-    relay_left = remote(
-        pair_sum(2, near, zl, [opposite_in.at[0], opposite_in.at[1]]), relay_in.at[1], XM
-    )
+    core_0f.wait_recv()
+    z_far0 = x_final_far(0)
+    core_1n = memory_terms(1, near)
     att_near_relay = near_relay(tok, att_in)
-    core_0f = memory_terms(0, far)
-    far_right.append(remote(pair_sum(1, far, 1 - zl), final_in.at[0, 1], XP))
-    out_terms(far, 0)
     core_3n = memory_terms(3, near)
-    target_terms(near, 2)
-    core_0f.wait_recv()
-    att_far = ring_far(tok, att_in, att_z, att_far_left, att_far_right)
-    z_far0 = x_final_far(0)
     core_1n.wait_recv()
     near_right = [remote(pair_sum(1, near, 1 - zl), final_in.at[0, 2], XP)]
     core_3n.wait_recv()
     near_left = [remote(pair_sum(3, near, 1 - zl), final_in.at[1, 2], XM)]
+    out_terms(far, 0)
+    target_terms(near, 2)
+    z_far1 = x_final_far(1)
+    att_far = ring_far(tok, att_in, att_z, att_far_left, att_far_right)
     tgt_near_relay = near_relay(cot, tgt_in)
+    for copy in (opposite_near, opposite_other, opposite_same):
+        copy.wait_recv()
+    pair_sum(2, near, zl, [opposite_in.at[0], opposite_in.at[1], opposite_in.at[2]])
+    relay_right = remote(half(2, 0), relay_in.at[0], XP)
+    relay_left = remote(half(2, 1), relay_in.at[1], XM)
     att_near_right = near_on_right(tok, att_in, out_terms)
     target_terms(far, 0)
     out_terms(near, 3)
     target_terms(near, 3)
+    pair_sum(1, near, zl)
+    pair_sum(3, near, zl)
     tgt_far_right = far_on_right(cot, tgt_in, tgt_far_relay)
-    z_far1 = x_final_far(1)
-    near_right.append(remote(pair_sum(1, near, zl), final_in.at[0, 3], XP))
+    relay_right.wait_recv()
+    add_rows(half(1, 0), [half(1, 0), relay_in.at[0]])
+    near_right.append(remote(part(1, near, zl), final_in.at[0, 3], XP))
     relay_left.wait_recv()
-    near_left.append(remote(pair_sum(3, near, zl, [relay_in.at[1]]), final_in.at[1, 3], XM))
+    add_rows(half(3, 1), [half(3, 1), relay_in.at[1]])
+    near_left.append(remote(part(3, near, zl), final_in.at[1, 3], XM))
     tgt_near_right = near_on_right(cot, tgt_in, target_terms)
     att_near_left = near_on_left(tok, att_in, att_near_relay)
     core_0n = memory_terms(0, near)
     out_terms(near, 0)
     target_terms(near, 0)
     core_0n.wait_recv()
+    z_near0 = x_final_near(0)
     tgt_near_left = near_on_left(cot, tgt_in, tgt_near_relay)
-    z_near0 = x_final_near(0)
     tgt_far = ring_far(cot, tgt_in, tgt_z, tgt_far_left, tgt_far_right)
     here = x_final_near(1)
     for copy in (z_far0, z_near0, z_far1):
@@ -524,8 +531,8 @@
         vmem((HEADS, TARGETS, MEMORY), BF16),
         vmem((HEADS, TARGETS, MEMORY), BF16),
         vmem((4, 128, D), BF16),
-        vmem((2, OWN_ROWS, SIDE), BF16),
-        vmem((2, OWN_ROWS, SIDE), BF16),
+        vmem((3, OWN_ROWS, SIDE), BF16),
+        vmem((2, OWN_ROWS // 2, SIDE), BF16),
         vmem((2, 4, OWN_ROWS, SIDE), BF16),
         vmem((3, OWN_ROWS, SIDE), BF16),
         vmem((3, OWN_ROWS, FEATURES), BF16),

time: 108 us -> 113 us (1.046)
  Pallas kernels: 107 us -> 112 us
    pallas_call x1, Pallas kernels: 105 us -> 110 us  [on_device(): pl.pallas_call(kernel, out_shape=(jax.ShapeDtypeStruct(tokens.shape, BF16...]
where the time goes in v4:
time: 113 us
  Pallas kernels  112 us (99%)
    pallas_call x1, Pallas kernels, on_device(): pl.pallas_call(kernel, out_shape=(jax.ShapeDtypeStruct(tokens.shape, BF16...  110 us

profile of v4, /device:TPU:1, one launch (start us, length us, event | category | flops | bytes accessed | tf_op | source)
XLA Modules:
  0.0 112.9 jit_solution(1719276458387446899)
XLA Ops:
  0.6 110.5 %shard_map.94 = (bf16[1,256,512]{2,1,0:T(8,128)(2,1)}, bf16[1,256,512]{2,1,0:T(8,128)(2,1)}, bf16[64,512]{1,0:T(8,128)(2,1)}) custom-call(bf16[1,256,512]{2,1,0:T(8,128)(2,1)} %tokens.1, bf16[1,256,512]{2,1,0:T(8,128)(2,1)} %cotangent.1, bf16[64,512]{1,0:T(8,128)(2,1)} %memory.1, bf16[1,4096,512]{2,1,0:T(8,128)(2,1)} %w_query.1, ...), custom_call_target="tpu_custom_call" | custom-call | flops 23000000512 | bytes 18874368 | tf_op jit(solution)/shard_map/pallas_call | solution.py:547
  111.1 1.9 %shard_map.95 = (bf16[1,256,512]{2,1,0:T(8,128)(2,1)}, bf16[1,256,512]{2,1,0:T(8,128)(2,1)}, bf16[64,512]{1,0:T(8,128)(2,1)}) custom-call(bf16[1,256,512]{2,1,0:T(8,128)(2,1)} %get-tuple-element.6.a_in, bf16[1,256,512]{2,1,0:T(8,128)(2,1)} %get-tuple-element.7.b_in, bf16[64,512]{1,0:T(8,128)(2,1)} %get-tuple-element.8.c_in), custom_call_target="tpu_custom_call" | custom-call | tf_op jit(solution)/shard_map/pallas_call | solution.py:562

commit v5 on v4

--- a/solution.py
+++ b/solution.py
@@ -171,12 +171,12 @@
     def arrive_x(dz):
         for copy in right[dz]:
             copy.wait_recv()
-        if dz == 0:
+        if dz in (0, 2):
             on_right[dz] = remote(piece(3, c, dz, 0), piece(3, c, dz, 0), XP)
         core_left[dz] = remote(piece(3, c, dz), piece(3, c, dz), CORE)
         for copy in left[dz]:
             copy.wait_recv()
-        if dz == 0:
+        if dz in (0, 2):
             on_left[dz] = remote(piece(1, c, dz, 1), piece(1, c, dz, 1), XM)
         core_right[dz] = remote(piece(1, c, dz), piece(1, c, dz), CORE)
 
@@ -237,7 +237,7 @@
 
     near_on = forward_targets(near, near_ring)
     arrive_opposite(0)
-    opposite_z = {dz: remote(piece(2, c, 0), piece(2, c, 0), dict(dz=dz)) for dz in (1, 3, 2)}
+    opposite_z = {dz: remote(piece(2, c, 0), piece(2, c, 0), dict(dz=dz)) for dz in (1, 3)}
     mem_z[2].wait_recv()
     spread(2)
     cot_z.wait_recv()
@@ -279,10 +279,10 @@
     far_g_on = remote(block(cot, far, 1), block(cot, far, 1), YM)
     far_on = (far_t_on, far_g_on)
     far_ring = (far_tok[0], far_cot[1], far_cot[0], far_tok[1])
-    arrive_opposite_z(2)
     for dz in (0, 1, 3, 2):
         core_right[dz].wait_recv()
     keys_values(1)
+    arrive_opposite(2)
     for dz in (0, 1, 3, 2):
         core_left[dz].wait_recv()
     keys_values(3)

time: 113 us -> 109 us (0.965)
  Pallas kernels: 112 us -> 108 us
    pallas_call x1, Pallas kernels: 110 us -> 107 us  [on_device(): pl.pallas_call(kernel, out_shape=(jax.ShapeDtypeStruct(tokens.shape, BF16...]
where the time goes in v5:
time: 109 us
  Pallas kernels  108 us (99%)
    pallas_call x1, Pallas kernels, on_device(): pl.pallas_call(kernel, out_shape=(jax.ShapeDtypeStruct(tokens.shape, BF16...  107 us

profile of v5, /device:TPU:1, one launch (start us, length us, event | category | flops | bytes accessed | tf_op | source)
XLA Modules:
  0.0 109.0 jit_solution(12320285207535640390)
XLA Ops:
  0.6 106.6 %shard_map.94 = (bf16[1,256,512]{2,1,0:T(8,128)(2,1)}, bf16[1,256,512]{2,1,0:T(8,128)(2,1)}, bf16[64,512]{1,0:T(8,128)(2,1)}) custom-call(bf16[1,256,512]{2,1,0:T(8,128)(2,1)} %tokens.1, bf16[1,256,512]{2,1,0:T(8,128)(2,1)} %cotangent.1, bf16[64,512]{1,0:T(8,128)(2,1)} %memory.1, bf16[1,4096,512]{2,1,0:T(8,128)(2,1)} %w_query.1, ...), custom_call_target="tpu_custom_call" | custom-call | flops 23000000512 | bytes 18874368 | tf_op jit(solution)/shard_map/pallas_call | solution.py:547
  107.2 1.9 %shard_map.95 = (bf16[1,256,512]{2,1,0:T(8,128)(2,1)}, bf16[1,256,512]{2,1,0:T(8,128)(2,1)}, bf16[64,512]{1,0:T(8,128)(2,1)}) custom-call(bf16[1,256,512]{2,1,0:T(8,128)(2,1)} %get-tuple-element.6.a_in, bf16[1,256,512]{2,1,0:T(8,128)(2,1)} %get-tuple-element.7.b_in, bf16[64,512]{1,0:T(8,128)(2,1)} %get-tuple-element.8.c_in), custom_call_target="tpu_custom_call" | custom-call | tf_op jit(solution)/shard_map/pallas_call | solution.py:562

commit v6 on v3

--- a/solution.py
+++ b/solution.py
@@ -130,11 +130,21 @@
 
     mem_y = {dy: remote(memory, own_mem, dict(dy=dy)) for dy in (1, 3, 2)}
     right, left, core_own, mem_z = {}, {}, {}, {}
+    def spread_targets():
+        t, g = tokens.at[0], cotangent.at[0]
+        t_dst, g_dst = block(tok, near, 0), block(cot, near, 0)
+        t_right = remote(t, t_dst, YP)
+        g_left = remote(g, g_dst, YM)
+        g_right = remote(g, g_dst, YP)
+        t_left = remote(t, t_dst, YM)
+        return t_right, g_left, g_right, t_left
+
     right[0] = [remote(memory, own_mem, XP)]
     left[0] = [remote(memory, own_mem, XM)]
     mem_z[1] = [remote(memory, own_mem, dict(dz=1))]
     mem_z[3] = [remote(memory, own_mem, dict(dz=3))]
     tok_z = remote(tokens.at[0], block(tok, near, 0), ZFAR)
+    near_ring = spread_targets()
     mem_load.wait()
     for dy in (1, 3, 2):
         mem_y[dy].wait_recv()
@@ -155,15 +165,6 @@
         left[dz] = [remote(here, here, XM)]
         core_own[dz] = remote(here, here, CORE)
 
-    def spread_targets():
-        t, g = tokens.at[0], cotangent.at[0]
-        t_dst, g_dst = block(tok, near, 0), block(cot, near, 0)
-        t_right = remote(t, t_dst, YP)
-        g_left = remote(g, g_dst, YM)
-        g_right = remote(g, g_dst, YP)
-        t_left = remote(t, t_dst, YM)
-        return t_right, g_left, g_right, t_left
-
     def spread_far(buf):
         here = block(buf, far, 0)
         return remote(here, here, YP), remote(here, here, YM)
@@ -199,7 +200,7 @@
         g_on = remote(block(cot, high, 1), block(cot, high, 1), YM)
         return t_on, g_on
 
-    def keys_values(dx):
+    def keys_values(dx, chunks=(0, 2)):
         to_x = x_at(dx)
         rows = aligned(to_x * 256, 256)
 
@@ -208,10 +209,9 @@
             kv[rows, cols] = dot(mem[to_x], wkv[:, cols]).astype(BF16)
             return 0
 
-        lax.fori_loop(0, 2, step, 0)
+        lax.fori_loop(chunks[0], chunks[1], step, 0)
 
     core_own[0] = remote(own, own, CORE)
-    near_ring = spread_targets()
     kv_loads, q_loads, o_loads = [], [], []
     for high in range(2):
         for row in range(4):
@@ -282,10 +282,11 @@
     for dz in (0, 1, 3, 2):
         core_right[dz].wait_recv()
     keys_values(1)
-    arrive_opposite(2)
     for dz in (0, 1, 3, 2):
         core_left[dz].wait_recv()
-    keys_values(3)
+    keys_values(3, (0, 1))
+    arrive_opposite(2)
+    keys_values(3, (1, 2))
     for dz in (0, 1, 3, 2):
         for copy in core_opposite[dz]:
             copy.wait_recv()

time: 108 us -> 108 us (level)
  no operation moved by 1% of the time
where the time goes in v6:
time: 108 us
  Pallas kernels  108 us (100%)
    pallas_call x1, Pallas kernels, on_device(): pl.pallas_call(kernel, out_shape=(jax.ShapeDtypeStruct(tokens.shape, BF16...  106 us

profile of v6, /device:TPU:1, one launch (start us, length us, event | category | flops | bytes accessed | tf_op | source)
XLA Modules:
  0.0 108.3 jit_solution(9189262265347514802)
XLA Ops:
  0.6 105.8 %shard_map.94 = (bf16[1,256,512]{2,1,0:T(8,128)(2,1)}, bf16[1,256,512]{2,1,0:T(8,128)(2,1)}, bf16[64,512]{1,0:T(8,128)(2,1)}) custom-call(bf16[1,256,512]{2,1,0:T(8,128)(2,1)} %tokens.1, bf16[1,256,512]{2,1,0:T(8,128)(2,1)} %cotangent.1, bf16[64,512]{1,0:T(8,128)(2,1)} %memory.1, bf16[1,4096,512]{2,1,0:T(8,128)(2,1)} %w_query.1, ...), custom_call_target="tpu_custom_call" | custom-call | flops 23000000512 | bytes 18874368 | tf_op jit(solution)/shard_map/pallas_call | solution.py:541
  106.4 1.9 %shard_map.95 = (bf16[1,256,512]{2,1,0:T(8,128)(2,1)}, bf16[1,256,512]{2,1,0:T(8,128)(2,1)}, bf16[64,512]{1,0:T(8,128)(2,1)}) custom-call(bf16[1,256,512]{2,1,0:T(8,128)(2,1)} %get-tuple-element.6.a_in, bf16[1,256,512]{2,1,0:T(8,128)(2,1)} %get-tuple-element.7.b_in, bf16[64,512]{1,0:T(8,128)(2,1)} %get-tuple-element.8.c_in), custom_call_target="tpu_custom_call" | custom-call | tf_op jit(solution)/shard_map/pallas_call | solution.py:556
